TPU v7x, 32 devices: a whole 2x2x4 slice. The times are simulated.
32 devices in a mesh: groups: 2 (over y), adapter: 8 (over z, x), tensor: 2 (over core).
Axes of the slice: x: 2, y: 2, z: 4, core: 2. Of those that a mesh axis runs over, the one named last changes fastest.
Arguments:
- layer_input: bfloat16 [256, 8192], P(('groups', 'adapter')), parts along dimension 0, may hold values from -6 to 6
- input_norm_gain: float32 [8192], replicated, may hold values from 0.5 to 1.5
- query_projection: bfloat16 [8192, 512], P(None, 'tensor'), may hold values from -0.0625 to 0.0625
- key_projection: bfloat16 [8192, 128], P(None, 'tensor'), may hold values from -0.0625 to 0.0625
- value_projection: bfloat16 [8192, 128], P(None, 'tensor'), may hold values from -0.0625 to 0.0625
- output_projection: bfloat16 [512, 8192], P('tensor'), may hold values from -1 to 1
- cached_key_rows: bfloat16 [256, 32, 128], P(('groups', 'adapter')), parts along dimension 0, may hold values from -120 to 120
- cached_value_rows: bfloat16 [256, 32, 128], P(('groups', 'adapter')), parts along dimension 0, may hold values from -6 to 6
- request_adapter: int32 [256, 1], P(('groups', 'adapter')), parts along dimension 0, may hold values from 0 to 7; in each aligned block of 16 rows (0 to 15, 16 to 31, ...) at most 4 rows name the same one
- adapter_row_table: int32 [8], replicated, may hold values from 0 to 7, each once
- cached_length: int32 [256], P(('groups', 'adapter')), parts along dimension 0, may hold values from 1 to 32, as said below
- projection_adapter_down: bfloat16 [8, 8192, 192], P('adapter', 'tensor'), may hold values from -0.0625 to 0.0625
- query_adapter_up: bfloat16 [8, 64, 512], P('adapter', None, 'tensor'), may hold values from -0.75 to 0.75
- key_value_adapter_up: bfloat16 [8, 2, 64, 128], P('adapter', None, None, 'tensor'), may hold values from -0.75 to 0.75
- output_adapter_down: bfloat16 [8, 512, 64], P('adapter', 'tensor'), may hold values from -1 to 1
- output_adapter_up: bfloat16 [8, 64, 8192], P('adapter', None, 'tensor'), may hold values from -0.75 to 0.75
Outputs:
- block_out: bfloat16 [256, 8192], P(('groups', 'adapter'), 'tensor'), parts along dimension 0
There are 2 independent parts, one for each index of `groups`. A program takes and returns all parts, laid end to end along the dimension named above; an argument that names none is the same for every part. Nothing has to cross between parts.
Inputs may be any that keep to these rules, and one draw needn't show every extreme that they name: `request_adapter`: among the requests of one device (aligned blocks of 16 rows) no adapter is named more than 4 times, a bound that some block reaches. A permutation: adapter j's weights are row adapter_row_table[j] of the adapter arrays. `cached_length`: the requests of every device include one whose cache holds exactly 32 positions.
All inputs are finite; a program needn't handle non-finite values.
Results may differ from a plain program's by a relative error of at most 0.012.
The roundings to bfloat16 on the way count: a program that leaves them out, or rounds other values in their place, can miss the bound.
Values may be sent and summed in bfloat16 or wider, within the bound.
No kernel may reach another device: no remote copies, remote signals or barrier semaphores. Data moves between devices by JAX's collectives and lax.ppermute only.
A program may use at most 64 MiB of HBM per device.

v0:
```python
import functools
import math

import jax
import jax.numpy as jnp
from jax import lax
from jax.experimental import pallas as pl
from jax.experimental.pallas import tpu as pltpu
from jax.sharding import PartitionSpec as P

HEAD_SIZE = 128
LANES = 128
EPSILON = 1e-05
THETA = 500000.0
BF16 = jnp.bfloat16
F32 = jnp.float32
SWAP = [(0, 1), (1, 0)]
GROUP = 16
MIB = 1024 * 1024


def nn(a, b):
    return lax.dot_general(a, b, (((1,), (0,)), ((), ())), preferred_element_type=F32)


def nt(a, b):
    return lax.dot_general(a, b, (((1,), (1,)), ((), ())), preferred_element_type=F32)


def iota(shape, dim):
    return lax.broadcasted_iota(jnp.int32, shape, dim)


def ones_where(condition):
    return jnp.where(condition, 1.0, 0.0).astype(BF16)


def owner_and_standing(named, table):
    requests, adapters = named.shape[1], table.shape[1]
    table_column = jnp.sum(
        jnp.where(iota((adapters, adapters), 0) == iota((adapters, adapters), 1), table, 0),
        axis=1,
        keepdims=True,
    )
    owner = jnp.sum(
        jnp.where(iota((adapters, requests), 0) == named, table_column, 0), axis=0, keepdims=True
    )
    square = (requests, requests)
    owner_column = jnp.sum(
        jnp.where(iota(square, 0) == iota(square, 1), owner, 0), axis=1, keepdims=True
    )
    earlier = (owner_column == owner) & (iota(square, 0) < iota(square, 1))
    standing = jnp.sum(jnp.where(earlier, 1, 0), axis=0, keepdims=True)
    return owner, standing


def copy_all(pairs, sems):
    copies = [pltpu.make_async_copy(a, b, sems.at[i]) for i, (a, b) in enumerate(pairs)]
    for copy in copies:
        copy.start()
    return copies


TURNS = ((1, 0, 2, 3), (0, 1, 2, 3))


def turn_of(distance, turns):
    turn = distance
    for n, one in enumerate(turns):
        turn = jnp.where(distance == one, n, turn)
    return turn


def block_of(ahead, core, count):
    ahead = jnp.where(ahead < 0, ahead + 2 * count, ahead)
    return jnp.where(ahead // count == core,
        jnp.where(
            core == 0,
            turn_of(count - 1 - ahead, TURNS[0]),
            turn_of(ahead - count, TURNS[1]),
        ), -1)


def pack_kernel(capacity, x_hbm, gain_hbm, k_hbm, v_hbm, named_hbm, table_hbm, length_hbm, *rest):
    x_ref, gain_ref, k_ref, v_ref, named_ref, table_ref, length_ref, flat_ref, spread_ref, sems = rest[-10:]
    blocks = rest[:-10]
    count = len(blocks)
    owners = 2 * count
    named_copy, table_copy, length_copy, x_copy, gain_copy, k_copy, v_copy = copy_all(
        [
            (named_hbm, named_ref),
            (table_hbm, table_ref),
            (length_hbm, length_ref),
            (x_hbm, x_ref),
            (gain_hbm, gain_ref),
            (k_hbm, k_ref),
            (v_hbm, v_ref),
        ],
        sems,
    )
    requests, width = x_ref.shape
    positions = k_ref.shape[0] // requests
    per_block = blocks[0].shape[0]
    rows = per_block * count
    named_copy.wait()
    table_copy.wait()
    length_copy.wait()
    owner, standing = owner_and_standing(named_ref[...], table_ref[...])
    block = block_of(owner - lax.axis_index("adapter"), lax.axis_index("tensor"), count)
    row = jnp.where(block < 0, -2, block * per_block + 2 * standing)
    order = iota((rows, requests), 0)
    put_x = ones_where(order == row)
    put_kv = ones_where(order == row + 1)
    put = jnp.concatenate([put_x, put_kv], axis=1)

    x_copy.wait()
    gain_copy.wait()
    floats = x_ref[...].astype(F32)
    scale = lax.rsqrt(jnp.mean(floats * floats, axis=1, keepdims=True) + EPSILON)
    flat_ref[0:requests, :] = (floats * scale * gain_ref[...]).astype(BF16)
    for n, (source, copy) in enumerate(((k_ref, k_copy), (v_ref, v_copy))):
        copy.wait()
        spread_ref[...] = source[...].astype(F32)
        for p in range(positions):
            to = slice((n * positions + p) * LANES, (n * positions + p + 1) * LANES)
            flat_ref[requests : 2 * requests, to] = spread_ref[
                pl.ds(p, requests, stride=positions), :
            ].astype(BF16)
    step = 1024
    for c in range(0, width, step):
        placed = nn(put, flat_ref[:, c : c + step]).astype(BF16)
        for j, block in enumerate(blocks):
            block[:, c : c + step] = placed[j * per_block : (j + 1) * per_block]
    square = (requests, requests)
    length_column = jnp.sum(
        jnp.where(iota(square, 0) == iota(square, 1), length_ref[...], 0), axis=1, keepdims=True
    )
    lengths = jnp.broadcast_to(length_column.astype(F32), (requests, LANES)).astype(BF16)
    placed = nn(put_x, lengths).astype(BF16)
    for j, block in enumerate(blocks):
        block[:, width:] = placed[j * per_block : (j + 1) * per_block]


def stacked(blocks, columns):
    return jnp.concatenate([block[:, columns] for block in blocks], axis=0)


def stage_kernel(wq_hbm, wk_hbm, wv_hbm, down_hbm, up_hbm, kv_up_hbm, out_down_hbm, out_up_hbm, wq_ref, narrow_ref, small_ref, up_ref, kv_up_ref, out_down_ref, sems):
    width = wq_hbm.shape[0]
    hcols = wk_hbm.shape[0]
    ranks = down_hbm.shape[0]
    pieces = 4
    pairs = [
        (up_hbm, up_ref),
        (kv_up_hbm, kv_up_ref),
        (out_down_hbm, out_down_ref),
        (out_up_hbm, small_ref.at[:, 0 : out_up_hbm.shape[1]]),
    ]
    for n in range(pieces):
        rows = pl.ds(n * (width // pieces), width // pieces)
        pairs.append((wq_hbm.at[rows, :], wq_ref.at[rows, :]))
    for n in range(2):
        rows = pl.ds(n * (ranks // 2), ranks // 2)
        pairs.append((down_hbm.at[rows, :], narrow_ref.at[pl.ds(4 * hcols + n * (ranks // 2), ranks // 2), :]))
        columns = pl.ds(n * (width // 2), width // 2)
        for m, source in enumerate((wk_hbm, wv_hbm)):
            target = narrow_ref.at[pl.ds((2 * n + m) * hcols, hcols), :]
            pairs.append((source.at[:, columns], target))
    copies = copy_all(pairs, sems)
    for copy in copies[:3]:
        copy.wait()
    small_ref[:, out_up_hbm.shape[1] :] = jnp.concatenate(
        [up_ref[...], kv_up_ref[0], kv_up_ref[1], out_down_ref[...]], axis=1
    )
    for copy in copies[3:]:
        copy.wait()


def project_kernel(count, *refs):
    blocks = refs[: 2 * count]
    wq_ref, narrow_ref, mine_ref, theirs_ref, sums_ref = refs[2 * count :]
    width = wq_ref.shape[0]
    half = narrow_ref.shape[1]
    slots = mine_ref.shape[0]
    rows = sums_ref.shape[1]
    kvcols = LANES
    x_all = stacked(blocks, slice(0, width))
    narrow = nt(jnp.concatenate([x_all[:, :half], x_all[:, half:]], axis=0), narrow_ref[...])
    early, late = narrow[:rows], narrow[rows:]
    ranks = jnp.where(lax.axis_index("tensor") == 0, early[:, 2 * kvcols :], late[:, 2 * kvcols :])
    spare = jnp.zeros((rows, -ranks.shape[1] % LANES), F32)
    sums = [
        nn(x_all, wq_ref[...]),
        early[:, :kvcols] + late[:, kvcols : 2 * kvcols],
        jnp.concatenate([ranks, spare], axis=1),
    ]
    tile = 0
    for part in sums:
        for c in range(0, part.shape[1], LANES):
            sums_ref[tile] = part[:, c : c + LANES]
            columns = slice(tile * LANES, (tile + 1) * LANES)
            mine_ref[:, columns] = sums_ref[tile, pl.ds(0, slots, stride=2), :]
            theirs_ref[:, columns] = sums_ref[tile, pl.ds(rows // 2, slots, stride=2), :]
            tile += 1


def unpack_kernel(count, *refs):
    blocks = refs[:count]
    named_ref, table_ref, k_ref, v_ref, length_ref, cosine_ref, sine_ref, place_ref = refs[count:]
    requests, rows = place_ref.shape
    core = lax.axis_index("tensor")
    owner, standing = owner_and_standing(named_ref[...], table_ref[...])
    ahead = owner - lax.axis_index("adapter")
    near, far = block_of(ahead, core, count), block_of(ahead, 1 - core, count)
    back = rows // (2 * count)
    source = jnp.where(near < 0, count + far, near) * back + core * (back // 2) + standing
    square = (requests, requests)
    source = jnp.sum(
        jnp.where(iota(square, 0) == iota(square, 1), source, 0), axis=1, keepdims=True
    )
    place_ref[...] = ones_where(iota((requests, rows), 1) == source)
    slots = length_ref.shape[0]
    per_block = blocks[0].shape[0]
    positions = k_ref.shape[0] // slots
    width = 2 * positions * LANES
    together = GROUP // (per_block // 2)
    pick = iota((GROUP, 2 * GROUP), 1) - 2 * iota((GROUP, 2 * GROUP), 0)
    pick_x, pick_kv = ones_where(pick == 0), ones_where(pick == 1)
    step = 1024
    for g in range(slots // GROUP):
        members = blocks[g * together : (g + 1) * together]
        for c in range(0, width, step):
            picked = nn(pick_kv, stacked(members, slice(c, c + step))).astype(BF16)
            for j in range(step // LANES):
                p = c // LANES + j
                target, p = (k_ref, p) if p < positions else (v_ref, p - positions)
                first = (g * positions + p) * GROUP
                target[first : first + GROUP, :] = picked[:, j * LANES : (j + 1) * LANES]
        length_ref[g * GROUP : (g + 1) * GROUP, :] = nn(
            pick_x, stacked(members, slice(width, width + LANES))
        )
    halfway = HEAD_SIZE // 2
    lane = iota((slots, LANES), 1)
    exponent = (lane % halfway).astype(F32) * (-math.log(THETA) / halfway)
    angle = length_ref[...] * jnp.exp(exponent)
    cosine_ref[...] = jnp.cos(angle)
    sine = jnp.sin(angle)
    sine_ref[...] = jnp.where(lane < halfway, -sine, sine)


def attend_kernel(mine_ref, theirs_ref, small_ref, small_other_ref, k_ref, v_ref, length_ref, cosine_ref, sine_ref, out_ref):
    core = lax.axis_index("tensor")
    slots = mine_ref.shape[0]
    rank = small_ref.shape[0]
    kvcols = LANES
    qcols = out_ref.shape[1] // 2
    heads = 2 * qcols // HEAD_SIZE
    halfway = HEAD_SIZE // 2
    both = qcols + kvcols
    base = small_ref.shape[1] - both - qcols
    mine = mine_ref[...]
    theirs = theirs_ref[...]
    ranks = (mine + theirs)[:, both : both + 3 * rank].astype(BF16)
    ranks = [ranks[:, n * rank : (n + 1) * rank] for n in range(3)]

    def added(projected, up_ref):
        change = jnp.concatenate(
            [
                nn(ranks[0], up_ref[:, base : base + qcols]),
                nn(ranks[1], up_ref[:, base + qcols : base + qcols + halfway]),
                nn(ranks[2], up_ref[:, base + qcols + halfway : base + both]),
            ],
            axis=1,
        )
        return projected[:, :both] + change.astype(BF16).astype(F32)

    mine = added(mine, small_ref)
    theirs = added(theirs, small_other_ref)
    combined = jnp.concatenate([mine[:, :qcols], theirs[:, :qcols]], axis=1)
    cosine, sine = cosine_ref[...], sine_ref[...]

    def rotate(part):
        return part * cosine + pltpu.roll(part, halfway, 1) * sine

    queries = [
        rotate(combined[:, h * HEAD_SIZE : (h + 1) * HEAD_SIZE]).astype(BF16) for h in range(heads)
    ]
    kv_mine = mine[:, qcols:]
    kv_theirs = theirs[:, qcols:]
    leading = jnp.where(core == 0, kv_mine, kv_theirs)
    trailing = jnp.where(core == 0, kv_theirs, kv_mine)
    first = iota((slots, LANES), 1) < halfway
    own_keys = rotate(jnp.where(first, leading, pltpu.roll(trailing, halfway, 1))).astype(BF16)
    own_values = jnp.where(first, pltpu.roll(leading, halfway, 1), trailing).astype(BF16)

    cached = k_ref.shape[0] * GROUP // slots
    rows = heads * GROUP
    shrink = math.sqrt(HEAD_SIZE)
    column = iota((rows, cached), 1)
    same = column % GROUP == iota((rows, cached), 0) % GROUP
    position = column // GROUP
    own = iota((rows, GROUP), 1) == iota((rows, GROUP), 0) % GROUP
    for g in range(slots // GROUP):
        members = slice(g * GROUP, (g + 1) * GROUP)
        held = slice(g * cached, (g + 1) * cached)
        query = jnp.concatenate([part[members] for part in queries], axis=0)
        length = jnp.concatenate([length_ref[members, 0:1]] * heads, axis=0).astype(jnp.int32)
        scores = jnp.where(
            same & (position < length), nt(query, k_ref[held, :]) / shrink, -jnp.inf
        )
        own_scores = jnp.where(own, nt(query, own_keys[members]) / shrink, -jnp.inf)
        highest = jnp.maximum(
            jnp.max(scores, axis=1, keepdims=True), jnp.max(own_scores, axis=1, keepdims=True)
        )
        raised = jnp.exp(scores - highest)
        own_raised = jnp.exp(own_scores - highest)
        total = jnp.sum(raised, axis=1, keepdims=True) + jnp.sum(own_raised, axis=1, keepdims=True)
        weights = (raised / total).astype(BF16)
        own_weights = (own_raised / total).astype(BF16)
        attended = (nn(weights, v_ref[held, :]) + nn(own_weights, own_values[members])).astype(BF16)
        for h in range(heads):
            out_ref[members, h * HEAD_SIZE : (h + 1) * HEAD_SIZE] = attended[
                h * GROUP : (h + 1) * GROUP
            ]


def output_kernel(count, attended_ref, wo_ref, wo_other_ref, small_ref, small_other_ref, *blocks):
    core = lax.axis_index("tensor")
    slots, cols = attended_ref.shape
    hcols = cols // 2
    per_block, half = blocks[0].shape
    kept = per_block // 2
    rows = count * per_block
    slot = iota((rows, slots), 0)
    slot = slot // per_block * kept + slot % kept
    attended = nn(ones_where(iota((rows, slots), 1) == slot), attended_ref[...]).astype(BF16)
    left, right = attended[:, :hcols], attended[:, hcols:]
    down = slice(small_ref.shape[1] - hcols, small_ref.shape[1])
    ranks = (nt(left, small_ref[:, down]) + nt(right, small_other_ref[:, down])).astype(BF16)
    step = 1024
    side = iota((rows, step), 0) % per_block // kept
    for c in range(0, half, step):
        near, far = slice(c, c + step), slice(half + c, half + c + step)
        terms = jnp.where(
            side == 0,
            nn(left, wo_ref[:, near]) + nn(right, wo_other_ref[:, near]),
            nn(left, wo_ref[:, far]) + nn(right, wo_other_ref[:, far]),
        )
        delta = jnp.where(side == core, nn(ranks, small_ref[:, near]), nn(ranks, small_other_ref[:, near]))
        done = (terms + delta.astype(BF16).astype(F32)).astype(BF16)
        for j, block in enumerate(blocks):
            block[:, near] = done[j * per_block : (j + 1) * per_block]


def pick_kernel(place_ref, *refs):
    blocks, out_ref = refs[:-1], refs[-1]
    step = 1024
    for c in range(0, out_ref.shape[1], step):
        out_ref[:, c : c + step] = nn(place_ref[...], stacked(blocks, slice(c, c + step))).astype(BF16)


OUTSIDE = pl.BlockSpec(memory_space=pltpu.HBM)
INSIDE = pl.BlockSpec(memory_space=pltpu.VMEM)


def call(kernel, outs, scratch=(), vmem=8, outside=(), out_spec=INSIDE, moved=0):
    many = isinstance(outs, (list, tuple))
    return lambda *args: pl.pallas_call(
        kernel,
        out_shape=outs,
        in_specs=[OUTSIDE if i in outside else INSIDE for i in range(len(args))],
        out_specs=[out_spec] * len(outs) if many else out_spec,
        scratch_shapes=list(scratch),
        compiler_params=pltpu.CompilerParams(vmem_limit_bytes=vmem * MIB),
        cost_estimate=pl.CostEstimate(flops=0, bytes_accessed=moved, transcendentals=0),
    )(
        *[
            pltpu.with_memory_space_constraint(arg, pltpu.HBM) if i in outside else arg
            for i, arg in enumerate(args)
        ]
    )


def body(
    layer_input,
    input_norm_gain,
    query_projection,
    key_projection,
    value_projection,
    output_projection,
    cached_key_rows,
    cached_value_rows,
    request_adapter,
    adapter_row_table,
    cached_length,
    projection_adapter_down,
    query_adapter_up,
    key_value_adapter_up,
    output_adapter_down,
    output_adapter_up,
):
    shape = jax.ShapeDtypeStruct
    requests, width = layer_input.shape
    owners = lax.axis_size("adapter")
    adapters = adapter_row_table.shape[0]
    positions = cached_key_rows.shape[1]
    half = width // 2
    capacity = max(2, 2 * ((requests + adapters - 1) // adapters))
    count = owners // 2
    kept = (capacity + 3) // 4 * 4
    slots = count * kept
    block = shape((2 * kept, width + LANES), BF16)
    named = request_adapter.reshape(1, requests)
    table = adapter_row_table.reshape(1, adapters)

    rank, qcols = query_adapter_up.shape[1:]
    hcols = key_value_adapter_up.shape[3]
    hrows = output_projection.shape[0]
    packed = call(
        functools.partial(pack_kernel, capacity),
        [block] * count,
        [
            pltpu.VMEM((requests, width), BF16),
            pltpu.VMEM((1, width), F32),
            pltpu.VMEM((positions * requests, LANES), BF16),
            pltpu.VMEM((positions * requests, LANES), BF16),
            pltpu.VMEM((1, requests), jnp.int32),
            pltpu.VMEM((1, adapters), jnp.int32),
            pltpu.VMEM((1, requests), jnp.int32),
            pltpu.VMEM((2 * requests, width), BF16),
            pltpu.VMEM((positions * requests, LANES), F32),
            pltpu.SemaphoreType.DMA((7,)),
        ],
        outside=range(7),
    )(
        layer_input,
        input_norm_gain.reshape(1, width),
        cached_key_rows.reshape(requests * positions, HEAD_SIZE),
        cached_value_rows.reshape(requests * positions, HEAD_SIZE),
        named,
        table,
        cached_length.reshape(1, requests),
    )
    down = projection_adapter_down[0].T
    wk, wv = key_projection.T, value_projection.T
    kvcols = 2 * wk.shape[0]
    *packed, query_projection, wk, wv, down = lax.optimization_barrier(
        (*packed, query_projection, wk, wv, down)
    )
    *weights, small = call(
        stage_kernel,
        [
            shape(query_projection.shape, BF16),
            shape((2 * kvcols + down.shape[0], half), BF16),
            shape((rank, half + qcols + 2 * hcols + hrows), BF16),
        ],
        [
            pltpu.VMEM((rank, qcols), BF16),
            pltpu.VMEM((2, rank, hcols), BF16),
            pltpu.VMEM((rank, hrows), BF16),
            pltpu.SemaphoreType.DMA((14,)),
        ],
        outside=range(8),
        moved=2 * (query_projection.size + kvcols * width + down.size),
    )(
        query_projection,
        wk,
        wv,
        down,
        query_adapter_up[0],
        key_value_adapter_up[0],
        output_adapter_down[0].T,
        output_adapter_up[0],
    )

    def onward(n):
        near, far = [turns[n] if n < len(turns) else n for turns in TURNS]
        shifts = (count - 1 - near, count + far)
        return [
            (a * 2 + t, (a + shifts[t]) % owners * 2 + t) for a in range(owners) for t in range(2)
        ]

    arrived = [
        lax.ppermute(one, ("adapter", "tensor"), onward(n)) for n, one in enumerate(packed)
    ]
    arrived[0], *weights = lax.optimization_barrier((arrived[0], *weights))
    passed = [lax.ppermute(one, "tensor", SWAP) for one in arrived]
    wo_other = lax.ppermute(output_projection, "tensor", SWAP)
    pcols = qcols + kvcols + (down.shape[0] + LANES - 1) // LANES * LANES
    mine, theirs = call(
        functools.partial(project_kernel, count),
        [shape((slots, pcols), F32), shape((slots, pcols), F32)],
        [pltpu.VMEM((pcols // LANES, 4 * slots, LANES), F32)],
        vmem=24,
    )(*arrived, *passed, *weights)
    theirs, mine, small = lax.optimization_barrier((theirs, mine, small))
    theirs = lax.ppermute(theirs, "tensor", SWAP)
    small_other = lax.ppermute(small, "tensor", SWAP)
    keys, values, lengths, cosine, sine, place = call(
        functools.partial(unpack_kernel, count),
        [shape((slots * positions, HEAD_SIZE), BF16)] * 2
        + [shape((slots, LANES), F32)] * 3
        + [shape((requests, 4 * slots), BF16)],
    )(*arrived, named, table)
    attended = call(attend_kernel, shape((slots, 2 * qcols), BF16), vmem=16)(
        mine, theirs, small, small_other, keys, values, lengths, cosine, sine
    )
    finished = call(
        functools.partial(output_kernel, count),
        [shape((2 * kept, half), BF16)] * count,
        vmem=16,
    )(attended, output_projection, wo_other, small, small_other)
    returned = [
        lax.ppermute(one, ("adapter", "tensor"), [(b, a) for a, b in onward(n)])
        for n, one in enumerate(finished)
    ]
    waited = list(returned)
    for n in reversed(range(count - 1)):
        waited[n] = lax.optimization_barrier((returned[n], returned[n + 1]))[0]
    returned += [lax.ppermute(one, "tensor", SWAP) for one in waited]
    return call(pick_kernel, shape((requests, half), BF16))(place, *returned)


def solution(mesh):
    placed = (
        P(("groups", "adapter"), None),
        P(),
        P(None, "tensor"),
        P(None, "tensor"),
        P(None, "tensor"),
        P("tensor", None),
        P(("groups", "adapter"), None, None),
        P(("groups", "adapter"), None, None),
        P(("groups", "adapter"), None),
        P(),
        P(("groups", "adapter")),
        P("adapter", "tensor", None),
        P("adapter", None, "tensor"),
        P("adapter", None, None, "tensor"),
        P("adapter", "tensor", None),
        P("adapter", None, "tensor"),
    )
    return jax.shard_map(
        body,
        mesh=mesh,
        in_specs=placed,
        out_specs=P(("groups", "adapter"), "tensor"),
        check_vma=False,
    )
```

profile of v0, /device:TPU:0, one launch (start us, length us, event | category | flops | bytes accessed | tf_op | source)
XLA Modules:
  0.0 39.2 jit_solution(2878099842829704865)
XLA Ops:
  0.0 0.5 %collective-permute-start.10 = (bf16[256,8192]{1,0:T(8,128)(2,1)}, bf16[256,8192]{1,0:T(8,128)(2,1)S(1)}, u32[]{:S(2)}, u32[]{:S(2)}) collective-permute-start(bf16[256,8192]{1,0:T(8,128)(2,1)} %wo_ref.1), channel_id=1, source_target_pairs={{0,1},{1,0},{2,3},{3,2},{4,5},{5,4},{6,7},{7,6},{8,9},{9,8},{10,11... | collective-permute-start | bytes 12582920 | tf_op jit(solution)/shard_map/ppermute | solution.py:488
  0.5 1.8 %shard_map.154 = (bf16[8,8320]{1,0:T(8,128)(2,1)S(1)}, bf16[8,8320]{1,0:T(8,128)(2,1)S(1)}, bf16[8,8320]{1,0:T(8,128)(2,1)S(1)}, bf16[8,8320]{1,0:T(8,128)(2,1)S(1)}) custom-call(bf16[16,8192]{1,0:T(8,128)(2,1)} %x_hbm.1, f32[1,8192]{1,0:T(1,128)} %bitcast.30, bf16[512,128]{1,0:T(8,128)(2,1)} %bitcast.25, bf16[512,128]{1,0:T(8,128)(2,1)} %bitcast.26, ...), custom_call_target="tpu_custom_call" | custom-call | tf_op jit(solution)/shard_map/pallas_call | solution.py:368
  2.3 2.6 %collective-permute-start = (bf16[8,8320]{1,0:T(8,128)(2,1)S(1)}, bf16[8,8320]{1,0:T(8,128)(2,1)S(1)}, u32[]{:S(2)}, u32[]{:S(2)}) collective-permute-start(bf16[8,8320]{1,0:T(8,128)(2,1)S(1)} %get-tuple-element.45), channel_id=1, source_target_pairs={{0,4},{1,9},{2,6},{3,11},{4,8},{5,13},{6,10},{7,15},{8,12},{9,1},{... | collective-permute-start | bytes 399368 | tf_op jit(solution)/shard_map/ppermute | solution.py:484
  4.9 2.5 %collective-permute-start.1 = (bf16[8,8320]{1,0:T(8,128)(2,1)S(1)}, bf16[8,8320]{1,0:T(8,128)(2,1)S(1)}, u32[]{:S(2)}, u32[]{:S(2)}) collective-permute-start(bf16[8,8320]{1,0:T(8,128)(2,1)S(1)} %get-tuple-element.53), channel_id=1, source_target_pairs={{0,6},{1,11},{2,8},{3,13},{4,10},{5,15},{6,12},{7,1},{8,14},{9,3},... | collective-permute-start | bytes 399368 | tf_op jit(solution)/shard_map/ppermute | solution.py:484
  7.4 1.5 %collective-permute-start.2 = (bf16[8,8320]{1,0:T(8,128)(2,1)S(1)}, bf16[8,8320]{1,0:T(8,128)(2,1)S(1)}, u32[]{:S(2)}, u32[]{:S(2)}) collective-permute-start(bf16[8,8320]{1,0:T(8,128)(2,1)S(1)} %get-tuple-element.54), channel_id=1, source_target_pairs={{0,2},{1,13},{2,4},{3,15},{4,6},{5,1},{6,8},{7,3},{8,10},{9,5},{10... | collective-permute-start | bytes 399368 | tf_op jit(solution)/shard_map/ppermute | solution.py:484
  9.0 0.7 %collective-permute-start.3 = (bf16[8,8320]{1,0:T(8,128)(2,1)S(1)}, bf16[8,8320]{1,0:T(8,128)(2,1)S(1)}, u32[]{:S(2)}, u32[]{:S(2)}) collective-permute-start(bf16[8,8320]{1,0:T(8,128)(2,1)S(1)} %get-tuple-element.55), channel_id=1, source_target_pairs={{0,0},{1,15},{2,2},{3,1},{4,4},{5,3},{6,6},{7,5},{8,8},{9,7},{10,1... | collective-permute-start | bytes 399368 | tf_op jit(solution)/shard_map/ppermute | solution.py:484
  9.6 3.6 %shard_map.155 = (bf16[8192,256]{1,0:T(8,128)(2,1)S(1)}, bf16[448,4096]{1,0:T(8,128)(2,1)S(1)}, bf16[64,4736]{1,0:T(8,128)(2,1)S(1)}) custom-call(bf16[8192,256]{1,0:T(8,128)(2,1)} %wq_hbm, bf16[64,8192]{1,0:T(8,128)(2,1)} %bitcast.22, bf16[64,8192]{1,0:T(8,128)(2,1)} %bitcast.23, bf16[192,4096]{1,0:T(8,128)(2,1)} %bitcast.21, bf16[64,256]{1,0:T(8,128)(2,1)} %bitcast.27, ...), custom_call_target="tpu_custom_call" | custom-call | bytes 7864320 | tf_op jit(solution)/shard_map/pallas_call | solution.py:368
  13.2 0.0 collective-permute-done.refs_0_
  13.2 0.0 copy-start.1
  13.2 0.0 copy-start.2
  13.2 0.0 copy-start
  13.2 3.1 %collective-permute-start.4 = (bf16[8,8320]{1,0:T(8,128)(2,1)S(1)}, bf16[8,8320]{1,0:T(8,128)(2,1)S(1)}, u32[]{:S(2)}, u32[]{:S(2)}) collective-permute-start(bf16[8,8320]{1,0:T(8,128)(2,1)S(1)} %collective-permute-done.refs_0_), channel_id=1, source_target_pairs={{0,1},{1,0},{2,3},{3,2},{4,5},{5,4},{6,7},{7,6},{8,9},{9,8},{10,11... | collective-permute-start | bytes 399368 | tf_op jit(solution)/shard_map/ppermute | solution.py:487
  16.3 1.7 %collective-permute-done.1.refs_1_ = bf16[8,8320]{1,0:T(8,128)(2,1)S(1)} collective-permute-done((bf16[8,8320]{1,0:T(8,128)(2,1)S(1)}, bf16[8,8320]{1,0:T(8,128)(2,1)S(1)}, u32[]{:S(2)}, u32[]{:S(2)}) %collective-permute-start.1) | collective-permute-done | bytes 133152 | tf_op jit(solution)/shard_map/ppermute | solution.py:484
  18.0 0.0 collective-permute-start.5
  18.0 0.0 collective-permute-done.2.refs_2_
  18.0 0.5 %collective-permute-start.6 = (bf16[8,8320]{1,0:T(8,128)(2,1)S(1)}, bf16[8,8320]{1,0:T(8,128)(2,1)S(1)}, u32[]{:S(2)}, u32[]{:S(2)}) collective-permute-start(bf16[8,8320]{1,0:T(8,128)(2,1)S(1)} %collective-permute-done.2.refs_2_), channel_id=1, source_target_pairs={{0,1},{1,0},{2,3},{3,2},{4,5},{5,4},{6,7},{7,6},{8,9},{9,8},{10,11... | collective-permute-start | bytes 399368 | tf_op jit(solution)/shard_map/ppermute | solution.py:487
  18.5 0.0 collective-permute-done.3.refs_3_
  18.5 0.1 collective-permute-start.7
  18.6 0.0 collective-permute-done.4.refs_4_
  18.6 0.8 %collective-permute-done.5.refs_5_ = bf16[8,8320]{1,0:T(8,128)(2,1)S(1)} collective-permute-done((bf16[8,8320]{1,0:T(8,128)(2,1)S(1)}, bf16[8,8320]{1,0:T(8,128)(2,1)S(1)}, u32[]{:S(2)}, u32[]{:S(2)}) %collective-permute-start.5) | collective-permute-done | bytes 133152 | tf_op jit(solution)/shard_map/ppermute | solution.py:487
  19.4 0.2 collective-permute-done.6.refs_6_
  19.5 0.3 collective-permute-done.7.refs_7_
  19.9 1.9 %shard_map.157 = (f32[16,640]{1,0:T(8,128)S(1)}, f32[16,640]{1,0:T(8,128)S(1)}) custom-call(bf16[8,8320]{1,0:T(8,128)(2,1)S(1)} %collective-permute-done.refs_0_, bf16[8,8320]{1,0:T(8,128)(2,1)S(1)} %collective-permute-done.1.refs_1_, bf16[8,8320]{1,0:T(8,128)(2,1)S(1)} %collective-permute-done.2.refs_2_, ...), custom_call_target="tpu_custom_call" | custom-call | tf_op jit(solution)/shard_map/pallas_call | solution.py:368
  21.8 0.3 collective-permute-start.9
  22.0 0.3 collective-permute-start.8
  22.3 0.3 shard_map.156
  22.6 1.3 %collective-permute-done.8.theirs_ref = f32[16,640]{1,0:T(8,128)S(1)} collective-permute-done((f32[16,640]{1,0:T(8,128)S(1)}, f32[16,640]{1,0:T(8,128)S(1)}, u32[]{:S(2)}, u32[]{:S(2)}) %collective-permute-start.8) | collective-permute-done | bytes 40992 | tf_op jit(solution)/shard_map/ppermute | solution.py:497
  23.9 0.0 collective-permute-done.9.small_other_ref
  23.9 0.9 %shard_map.158.attended_ref = bf16[16,512]{1,0:T(8,128)(2,1)S(1)} custom-call(f32[16,640]{1,0:T(8,128)S(1)} %get-tuple-element.62.mine_ref, f32[16,640]{1,0:T(8,128)S(1)} %collective-permute-done.8.theirs_ref, bf16[64,4736]{1,0:T(8,128)(2,1)S(1)} %get-tuple-element.64.small_ref, bf16[64,4736]{1,0:T(8,128)(2,1)S(1)} %collective-permute-done.9.small_other_ref, ...), custom_call_target="tpu_custom_call" | custom-call | tf_op jit(solution)/shard_map/pallas_call | solution.py:368
  24.8 0.0 collective-permute-done.10.wo_other_ref
  24.8 1.5 %shard_map.159 = (bf16[8,4096]{1,0:T(8,128)(2,1)S(1)}, bf16[8,4096]{1,0:T(8,128)(2,1)S(1)}, bf16[8,4096]{1,0:T(8,128)(2,1)S(1)}, bf16[8,4096]{1,0:T(8,128)(2,1)S(1)}) custom-call(bf16[16,512]{1,0:T(8,128)(2,1)S(1)} %shard_map.158.attended_ref, bf16[256,8192]{1,0:T(8,128)(2,1)S(1)} %copy-done, bf16[256,8192]{1,0:T(8,128)(2,1)S(1)} %collective-permute-done.10.wo_other_ref, ...), custom_call_target="tpu_custom_call" | custom-call | tf_op jit(solution)/shard_map/pallas_call | solution.py:368
  26.3 4.2 %collective-permute-start.13 = (bf16[8,4096]{1,0:T(8,128)(2,1)S(1)}, bf16[8,4096]{1,0:T(8,128)(2,1)S(1)}, u32[]{:S(2)}, u32[]{:S(2)}) collective-permute-start(bf16[8,4096]{1,0:T(8,128)(2,1)S(1)} %get-tuple-element.72), channel_id=1, source_target_pairs={{2,0},{13,1},{4,2},{15,3},{6,4},{1,5},{8,6},{3,7},{10,8},{5,9},{12... | collective-permute-start | bytes 196616 | tf_op jit(solution)/shard_map/ppermute | solution.py:514
  30.6 0.7 %collective-permute-start.14 = (bf16[8,4096]{1,0:T(8,128)(2,1)S(1)}, bf16[8,4096]{1,0:T(8,128)(2,1)S(1)}, u32[]{:S(2)}, u32[]{:S(2)}) collective-permute-start(bf16[8,4096]{1,0:T(8,128)(2,1)S(1)} %get-tuple-element.73), channel_id=1, source_target_pairs={{0,0},{15,1},{2,2},{1,3},{4,4},{3,5},{6,6},{5,7},{8,8},{7,9},{10,1... | collective-permute-start | bytes 196616 | tf_op jit(solution)/shard_map/ppermute | solution.py:514
  31.2 0.8 %collective-permute-start.12 = (bf16[8,4096]{1,0:T(8,128)(2,1)S(1)}, bf16[8,4096]{1,0:T(8,128)(2,1)S(1)}, u32[]{:S(2)}, u32[]{:S(2)}) collective-permute-start(bf16[8,4096]{1,0:T(8,128)(2,1)S(1)} %get-tuple-element.71), channel_id=1, source_target_pairs={{6,0},{11,1},{8,2},{13,3},{10,4},{15,5},{12,6},{1,7},{14,8},{3,9},... | collective-permute-start | bytes 196616 | tf_op jit(solution)/shard_map/ppermute | solution.py:514
  32.1 0.0 collective-permute-start.11
  32.1 0.4 %collective-permute-done.13.refs_2_ = bf16[8,4096]{1,0:T(8,128)(2,1)S(1)} collective-permute-done((bf16[8,4096]{1,0:T(8,128)(2,1)S(1)}, bf16[8,4096]{1,0:T(8,128)(2,1)S(1)}, u32[]{:S(2)}, u32[]{:S(2)}) %collective-permute-start.13) | collective-permute-done | bytes 65568 | tf_op jit(solution)/shard_map/ppermute | solution.py:514
  32.5 0.0 collective-permute-done.14.refs_3_
  32.5 3.0 %collective-permute-start.17 = (bf16[8,4096]{1,0:T(8,128)(2,1)S(1)}, bf16[8,4096]{1,0:T(8,128)(2,1)S(1)}, u32[]{:S(2)}, u32[]{:S(2)}) collective-permute-start(bf16[8,4096]{1,0:T(8,128)(2,1)S(1)} %collective-permute-done.13.refs_2_), channel_id=1, source_target_pairs={{0,1},{1,0},{2,3},{3,2},{4,5},{5,4},{6,7},{7,6},{8,9},{9,8},{10,11... | collective-permute-start | bytes 196616 | tf_op jit(solution)/shard_map/ppermute | solution.py:520
  35.5 1.1 %collective-permute-done.12.refs_1_ = bf16[8,4096]{1,0:T(8,128)(2,1)S(1)} collective-permute-done((bf16[8,4096]{1,0:T(8,128)(2,1)S(1)}, bf16[8,4096]{1,0:T(8,128)(2,1)S(1)}, u32[]{:S(2)}, u32[]{:S(2)}) %collective-permute-start.12) | collective-permute-done | bytes 65568 | tf_op jit(solution)/shard_map/ppermute | solution.py:514
  36.5 0.0 collective-permute-start.16
  36.5 0.0 collective-permute-done.11.refs_0_
  36.5 0.6 %collective-permute-start.15 = (bf16[8,4096]{1,0:T(8,128)(2,1)S(1)}, bf16[8,4096]{1,0:T(8,128)(2,1)S(1)}, u32[]{:S(2)}, u32[]{:S(2)}) collective-permute-start(bf16[8,4096]{1,0:T(8,128)(2,1)S(1)} %collective-permute-done.11.refs_0_), channel_id=1, source_target_pairs={{0,1},{1,0},{2,3},{3,2},{4,5},{5,4},{6,7},{7,6},{8,9},{9,8},{10,11... | collective-permute-start | bytes 196616 | tf_op jit(solution)/shard_map/ppermute | solution.py:520
  37.1 0.0 collective-permute-start.18
  37.1 0.0 collective-permute-done.17.refs_6_
  37.1 0.7 %collective-permute-done.16.refs_5_ = bf16[8,4096]{1,0:T(8,128)(2,1)S(1)} collective-permute-done((bf16[8,4096]{1,0:T(8,128)(2,1)S(1)}, bf16[8,4096]{1,0:T(8,128)(2,1)S(1)}, u32[]{:S(2)}, u32[]{:S(2)}) %collective-permute-start.16) | collective-permute-done | bytes 65568 | tf_op jit(solution)/shard_map/ppermute | solution.py:520
  37.8 0.2 collective-permute-done.15.refs_4_
  38.0 0.4 collective-permute-done.18.refs_7_
  38.4 0.9 %shard_map.160 = bf16[16,4096]{1,0:T(8,128)(2,1)} custom-call(bf16[16,64]{1,0:T(8,128)(2,1)S(1)} %get-tuple-element.56.place_ref, bf16[8,4096]{1,0:T(8,128)(2,1)S(1)} %collective-permute-done.11.refs_0_, bf16[8,4096]{1,0:T(8,128)(2,1)S(1)} %collective-permute-done.12.refs_1_, bf16[8,4096]{1,0:T(8,128)(2,1)S(1)} %collective-permute-done.13.refs_2_, ...), custom_call_target="tpu_custom_call" | custom-call | tf_op jit(solution)/shard_map/pallas_call | solution.py:368
  (3 shorter events, 0.0 us)
Async XLA Ops:
  0.0 24.8 %collective-permute-start.10 = (bf16[256,8192]{1,0:T(8,128)(2,1)}, bf16[256,8192]{1,0:T(8,128)(2,1)S(1)}, u32[]{:S(2)}, u32[]{:S(2)}) collective-permute-start(bf16[256,8192]{1,0:T(8,128)(2,1)} %wo_ref.1), channel_id=1, source_target_pairs={{0,1},{1,0},{2,3},{3,2},{4,5},{5,4},{6,7},{7,6},{8,9},{9,8},{10,11... | collective-permute-start | bytes 12582920 | tf_op jit(solution)/shard_map/ppermute | solution.py:488
  2.3 10.9 %collective-permute-start = (bf16[8,8320]{1,0:T(8,128)(2,1)S(1)}, bf16[8,8320]{1,0:T(8,128)(2,1)S(1)}, u32[]{:S(2)}, u32[]{:S(2)}) collective-permute-start(bf16[8,8320]{1,0:T(8,128)(2,1)S(1)} %get-tuple-element.45), channel_id=1, source_target_pairs={{0,4},{1,9},{2,6},{3,11},{4,8},{5,13},{6,10},{7,15},{8,12},{9,1},{... | collective-permute-start | bytes 399368 | tf_op jit(solution)/shard_map/ppermute | solution.py:484
  4.9 13.1 %collective-permute-start.1 = (bf16[8,8320]{1,0:T(8,128)(2,1)S(1)}, bf16[8,8320]{1,0:T(8,128)(2,1)S(1)}, u32[]{:S(2)}, u32[]{:S(2)}) collective-permute-start(bf16[8,8320]{1,0:T(8,128)(2,1)S(1)} %get-tuple-element.53), channel_id=1, source_target_pairs={{0,6},{1,11},{2,8},{3,13},{4,10},{5,15},{6,12},{7,1},{8,14},{9,3},... | collective-permute-start | bytes 399368 | tf_op jit(solution)/shard_map/ppermute | solution.py:484
  7.4 10.6 %collective-permute-start.2 = (bf16[8,8320]{1,0:T(8,128)(2,1)S(1)}, bf16[8,8320]{1,0:T(8,128)(2,1)S(1)}, u32[]{:S(2)}, u32[]{:S(2)}) collective-permute-start(bf16[8,8320]{1,0:T(8,128)(2,1)S(1)} %get-tuple-element.54), channel_id=1, source_target_pairs={{0,2},{1,13},{2,4},{3,15},{4,6},{5,1},{6,8},{7,3},{8,10},{9,5},{10... | collective-permute-start | bytes 399368 | tf_op jit(solution)/shard_map/ppermute | solution.py:484
  9.0 9.5 %collective-permute-start.3 = (bf16[8,8320]{1,0:T(8,128)(2,1)S(1)}, bf16[8,8320]{1,0:T(8,128)(2,1)S(1)}, u32[]{:S(2)}, u32[]{:S(2)}) collective-permute-start(bf16[8,8320]{1,0:T(8,128)(2,1)S(1)} %get-tuple-element.55), channel_id=1, source_target_pairs={{0,0},{1,15},{2,2},{3,1},{4,4},{5,3},{6,6},{7,5},{8,8},{9,7},{10,1... | collective-permute-start | bytes 399368 | tf_op jit(solution)/shard_map/ppermute | solution.py:484
  13.2 9.1 %copy-start.1 = (s32[16,1]{0,1:T(1,128)S(1)}, s32[16,1]{0,1:T(1,128)}, u32[]{:S(2)}) copy-start(s32[16,1]{0,1:T(1,128)} %param.24) | copy-start | bytes 196
  13.2 9.1 %copy-start.2 = (s32[8]{0:T(128)S(1)}, s32[8]{0:T(128)}, u32[]{:S(2)}) copy-start(s32[8]{0:T(128)} %param.25) | copy-start | bytes 100
  13.2 11.6 %copy-start = (bf16[256,8192]{1,0:T(8,128)(2,1)S(1)}, bf16[256,8192]{1,0:T(8,128)(2,1)}, u32[]{:S(2)}) copy-start(bf16[256,8192]{1,0:T(8,128)(2,1)} %wo_ref.1) | copy-start | bytes 12582916
  13.2 5.3 %collective-permute-start.4 = (bf16[8,8320]{1,0:T(8,128)(2,1)S(1)}, bf16[8,8320]{1,0:T(8,128)(2,1)S(1)}, u32[]{:S(2)}, u32[]{:S(2)}) collective-permute-start(bf16[8,8320]{1,0:T(8,128)(2,1)S(1)} %collective-permute-done.refs_0_), channel_id=1, source_target_pairs={{0,1},{1,0},{2,3},{3,2},{4,5},{5,4},{6,7},{7,6},{8,9},{9,8},{10,11... | collective-permute-start | bytes 399368 | tf_op jit(solution)/shard_map/ppermute | solution.py:487
  18.0 1.4 %collective-permute-start.5 = (bf16[8,8320]{1,0:T(8,128)(2,1)S(1)}, bf16[8,8320]{1,0:T(8,128)(2,1)S(1)}, u32[]{:S(2)}, u32[]{:S(2)}) collective-permute-start(bf16[8,8320]{1,0:T(8,128)(2,1)S(1)} %collective-permute-done.1.refs_1_), channel_id=1, source_target_pairs={{0,1},{1,0},{2,3},{3,2},{4,5},{5,4},{6,7},{7,6},{8,9},{9,8},{10,11... | collective-permute-start | bytes 399368 | tf_op jit(solution)/shard_map/ppermute | solution.py:487
  18.0 1.5 %collective-permute-start.6 = (bf16[8,8320]{1,0:T(8,128)(2,1)S(1)}, bf16[8,8320]{1,0:T(8,128)(2,1)S(1)}, u32[]{:S(2)}, u32[]{:S(2)}) collective-permute-start(bf16[8,8320]{1,0:T(8,128)(2,1)S(1)} %collective-permute-done.2.refs_2_), channel_id=1, source_target_pairs={{0,1},{1,0},{2,3},{3,2},{4,5},{5,4},{6,7},{7,6},{8,9},{9,8},{10,11... | collective-permute-start | bytes 399368 | tf_op jit(solution)/shard_map/ppermute | solution.py:487
  18.5 1.4 %collective-permute-start.7 = (bf16[8,8320]{1,0:T(8,128)(2,1)S(1)}, bf16[8,8320]{1,0:T(8,128)(2,1)S(1)}, u32[]{:S(2)}, u32[]{:S(2)}) collective-permute-start(bf16[8,8320]{1,0:T(8,128)(2,1)S(1)} %collective-permute-done.3.refs_3_), channel_id=1, source_target_pairs={{0,1},{1,0},{2,3},{3,2},{4,5},{5,4},{6,7},{7,6},{8,9},{9,8},{10,11... | collective-permute-start | bytes 399368 | tf_op jit(solution)/shard_map/ppermute | solution.py:487
  21.8 2.2 %collective-permute-start.9 = (bf16[64,4736]{1,0:T(8,128)(2,1)S(1)}, bf16[64,4736]{1,0:T(8,128)(2,1)S(1)}, u32[]{:S(2)}, u32[]{:S(2)}) collective-permute-start(bf16[64,4736]{1,0:T(8,128)(2,1)S(1)} %get-tuple-element.64.small_ref), channel_id=1, source_target_pairs={{0,1},{1,0},{2,3},{3,2},{4,5},{5,4},{6,7},{7,6},{8,9},{9,8},{10,11... | collective-permute-start | bytes 1818632 | tf_op jit(solution)/shard_map/ppermute | solution.py:498
  22.0 1.9 %collective-permute-start.8 = (f32[16,640]{1,0:T(8,128)S(1)}, f32[16,640]{1,0:T(8,128)S(1)}, u32[]{:S(2)}, u32[]{:S(2)}) collective-permute-start(f32[16,640]{1,0:T(8,128)S(1)} %get-tuple-element.63), channel_id=1, source_target_pairs={{0,1},{1,0},{2,3},{3,2},{4,5},{5,4},{6,7},{7,6},{8,9},{9,8},{10,11... | collective-permute-start | bytes 122888 | tf_op jit(solution)/shard_map/ppermute | solution.py:497
  26.3 6.2 %collective-permute-start.13 = (bf16[8,4096]{1,0:T(8,128)(2,1)S(1)}, bf16[8,4096]{1,0:T(8,128)(2,1)S(1)}, u32[]{:S(2)}, u32[]{:S(2)}) collective-permute-start(bf16[8,4096]{1,0:T(8,128)(2,1)S(1)} %get-tuple-element.72), channel_id=1, source_target_pairs={{2,0},{13,1},{4,2},{15,3},{6,4},{1,5},{8,6},{3,7},{10,8},{5,9},{12... | collective-permute-start | bytes 196616 | tf_op jit(solution)/shard_map/ppermute | solution.py:514
  30.6 1.9 %collective-permute-start.14 = (bf16[8,4096]{1,0:T(8,128)(2,1)S(1)}, bf16[8,4096]{1,0:T(8,128)(2,1)S(1)}, u32[]{:S(2)}, u32[]{:S(2)}) collective-permute-start(bf16[8,4096]{1,0:T(8,128)(2,1)S(1)} %get-tuple-element.73), channel_id=1, source_target_pairs={{0,0},{15,1},{2,2},{1,3},{4,4},{3,5},{6,6},{5,7},{8,8},{7,9},{10,1... | collective-permute-start | bytes 196616 | tf_op jit(solution)/shard_map/ppermute | solution.py:514
  31.2 5.3 %collective-permute-start.12 = (bf16[8,4096]{1,0:T(8,128)(2,1)S(1)}, bf16[8,4096]{1,0:T(8,128)(2,1)S(1)}, u32[]{:S(2)}, u32[]{:S(2)}) collective-permute-start(bf16[8,4096]{1,0:T(8,128)(2,1)S(1)} %get-tuple-element.71), channel_id=1, source_target_pairs={{6,0},{11,1},{8,2},{13,3},{10,4},{15,5},{12,6},{1,7},{14,8},{3,9},... | collective-permute-start | bytes 196616 | tf_op jit(solution)/shard_map/ppermute | solution.py:514
  32.1 4.5 %collective-permute-start.11 = (bf16[8,4096]{1,0:T(8,128)(2,1)S(1)}, bf16[8,4096]{1,0:T(8,128)(2,1)S(1)}, u32[]{:S(2)}, u32[]{:S(2)}) collective-permute-start(bf16[8,4096]{1,0:T(8,128)(2,1)S(1)} %get-tuple-element.70), channel_id=1, source_target_pairs={{4,0},{9,1},{6,2},{11,3},{8,4},{13,5},{10,6},{15,7},{12,8},{1,9},{... | collective-permute-start | bytes 196616 | tf_op jit(solution)/shard_map/ppermute | solution.py:514
  32.5 4.6 %collective-permute-start.17 = (bf16[8,4096]{1,0:T(8,128)(2,1)S(1)}, bf16[8,4096]{1,0:T(8,128)(2,1)S(1)}, u32[]{:S(2)}, u32[]{:S(2)}) collective-permute-start(bf16[8,4096]{1,0:T(8,128)(2,1)S(1)} %collective-permute-done.13.refs_2_), channel_id=1, source_target_pairs={{0,1},{1,0},{2,3},{3,2},{4,5},{5,4},{6,7},{7,6},{8,9},{9,8},{10,11... | collective-permute-start | bytes 196616 | tf_op jit(solution)/shard_map/ppermute | solution.py:520
  36.5 1.3 %collective-permute-start.16 = (bf16[8,4096]{1,0:T(8,128)(2,1)S(1)}, bf16[8,4096]{1,0:T(8,128)(2,1)S(1)}, u32[]{:S(2)}, u32[]{:S(2)}) collective-permute-start(bf16[8,4096]{1,0:T(8,128)(2,1)S(1)} %collective-permute-done.12.refs_1_), channel_id=1, source_target_pairs={{0,1},{1,0},{2,3},{3,2},{4,5},{5,4},{6,7},{7,6},{8,9},{9,8},{10,11... | collective-permute-start | bytes 196616 | tf_op jit(solution)/shard_map/ppermute | solution.py:520
  36.5 1.5 %collective-permute-start.15 = (bf16[8,4096]{1,0:T(8,128)(2,1)S(1)}, bf16[8,4096]{1,0:T(8,128)(2,1)S(1)}, u32[]{:S(2)}, u32[]{:S(2)}) collective-permute-start(bf16[8,4096]{1,0:T(8,128)(2,1)S(1)} %collective-permute-done.11.refs_0_), channel_id=1, source_target_pairs={{0,1},{1,0},{2,3},{3,2},{4,5},{5,4},{6,7},{7,6},{8,9},{9,8},{10,11... | collective-permute-start | bytes 196616 | tf_op jit(solution)/shard_map/ppermute | solution.py:520
  37.1 1.3 %collective-permute-start.18 = (bf16[8,4096]{1,0:T(8,128)(2,1)S(1)}, bf16[8,4096]{1,0:T(8,128)(2,1)S(1)}, u32[]{:S(2)}, u32[]{:S(2)}) collective-permute-start(bf16[8,4096]{1,0:T(8,128)(2,1)S(1)} %collective-permute-done.14.refs_3_), channel_id=1, source_target_pairs={{0,1},{1,0},{2,3},{3,2},{4,5},{5,4},{6,7},{7,6},{8,9},{9,8},{10,11... | collective-permute-start | bytes 196616 | tf_op jit(solution)/shard_map/ppermute | solution.py:520
where the time goes:
time: 39.5 us; the launch traced here: 39.2 us
  starting transfers between devices  21.3 us (54%)
  Pallas kernels  10.8 us (27%)
  waiting for transfers between devices  7.05 us (18%)
    pallas_call x7, Pallas kernels, call(): pl.pallas_call(kernel, out_shape=outs, in_specs=[OUTSIDE if i in outside...  10.8 us
    ppermute x4, starting transfers between devices, body(): lax.ppermute(one, ('adapter', 'tensor'), onward(n))  7.34 us
    ppermute x4, starting transfers between devices, body(): lax.ppermute(one, ('adapter', 'tensor'), [(b, a) for a, b in onward(n)])  5.72 us
    ppermute x4, starting transfers between devices, body(): passed = [lax.ppermute(one, 'tensor', SWAP) for one in arrived]  3.63 us
    ppermute x4, starting transfers between devices, body(): returned += [lax.ppermute(one, 'tensor', SWAP) for one in waited]  3.53 us
    ppermute x4, waiting for transfers between devices, body(): lax.ppermute(one, ('adapter', 'tensor'), onward(n))  1.71 us
    ppermute x4, waiting for transfers between devices, body(): lax.ppermute(one, ('adapter', 'tensor'), [(b, a) for a, b in onward(n)])  1.51 us
    ppermute x1, waiting for transfers between devices, body(): theirs = lax.ppermute(theirs, 'tensor', SWAP)  1.29 us
  transfers between devices with their start and end apart: 19, of which 10 were waited for; matrix products, arithmetic and copies ran while one was open for 0% of the time, Pallas kernels for 21%

commit v1 on v0

--- a/solution.py
+++ b/solution.py
@@ -61,7 +61,7 @@
     return copies
 
 
-TURNS = ((1, 0, 2, 3), (0, 1, 2, 3))
+TURNS = ((1, 0, 2, 3), (0, 1, 3, 2))
 
 
 def turn_of(distance, turns):
@@ -126,7 +126,7 @@
             flat_ref[requests : 2 * requests, to] = spread_ref[
                 pl.ds(p, requests, stride=positions), :
             ].astype(BF16)
-    step = 1024
+    step = 2048
     for c in range(0, width, step):
         placed = nn(put, flat_ref[:, c : c + step]).astype(BF16)
         for j, block in enumerate(blocks):
@@ -226,7 +226,7 @@
     together = GROUP // (per_block // 2)
     pick = iota((GROUP, 2 * GROUP), 1) - 2 * iota((GROUP, 2 * GROUP), 0)
     pick_x, pick_kv = ones_where(pick == 0), ones_where(pick == 1)
-    step = 1024
+    step = 2048
     for g in range(slots // GROUP):
         members = blocks[g * together : (g + 1) * together]
         for c in range(0, width, step):
@@ -337,7 +337,7 @@
     left, right = attended[:, :hcols], attended[:, hcols:]
     down = slice(small_ref.shape[1] - hcols, small_ref.shape[1])
     ranks = (nt(left, small_ref[:, down]) + nt(right, small_other_ref[:, down])).astype(BF16)
-    step = 1024
+    step = 2048
     side = iota((rows, step), 0) % per_block // kept
     for c in range(0, half, step):
         near, far = slice(c, c + step), slice(half + c, half + c + step)
@@ -354,7 +354,7 @@
 
 def pick_kernel(place_ref, *refs):
     blocks, out_ref = refs[:-1], refs[-1]
-    step = 1024
+    step = 2048
     for c in range(0, out_ref.shape[1], step):
         out_ref[:, c : c + step] = nn(place_ref[...], stacked(blocks, slice(c, c + step))).astype(BF16)
 

time: 39.5 us -> 39.5 us (level)
  starting transfers between devices: 21.3 us -> 20.9 us
where the time goes in v1:
time: 39.5 us; the launch traced here: 39.2 us
  starting transfers between devices  20.9 us (53%)
  Pallas kernels  10.8 us (27%)
  waiting for transfers between devices  7.4 us (19%)
    pallas_call x7, Pallas kernels, call(): pl.pallas_call(kernel, out_shape=outs, in_specs=[OUTSIDE if i in outside...  10.8 us
    ppermute x4, starting transfers between devices, body(): lax.ppermute(one, ('adapter', 'tensor'), onward(n))  7.34 us
    ppermute x4, starting transfers between devices, body(): lax.ppermute(one, ('adapter', 'tensor'), [(b, a) for a, b in onward(n)])  5.72 us
    ppermute x4, starting transfers between devices, body(): passed = [lax.ppermute(one, 'tensor', SWAP) for one in arrived]  3.63 us
    ppermute x4, starting transfers between devices, body(): returned += [lax.ppermute(one, 'tensor', SWAP) for one in waited]  3.17 us
    ppermute x4, waiting for transfers between devices, body(): lax.ppermute(one, ('adapter', 'tensor'), [(b, a) for a, b in onward(n)])  1.86 us
    ppermute x4, waiting for transfers between devices, body(): lax.ppermute(one, ('adapter', 'tensor'), onward(n))  1.71 us
    ppermute x1, waiting for transfers between devices, body(): theirs = lax.ppermute(theirs, 'tensor', SWAP)  1.29 us
  transfers between devices with their start and end apart: 19, of which 10 were waited for; matrix products, arithmetic and copies ran while one was open for 0% of the time, Pallas kernels for 21%

profile of v1, /device:TPU:0, one launch (start us, length us, event | category | flops | bytes accessed | tf_op | source)
XLA Modules:
  0.0 39.2 jit_solution(12551645022197388317)
XLA Ops:
  0.0 0.5 %collective-permute-start.10 = (bf16[256,8192]{1,0:T(8,128)(2,1)}, bf16[256,8192]{1,0:T(8,128)(2,1)S(1)}, u32[]{:S(2)}, u32[]{:S(2)}) collective-permute-start(bf16[256,8192]{1,0:T(8,128)(2,1)} %wo_ref.1), channel_id=1, source_target_pairs={{0,1},{1,0},{2,3},{3,2},{4,5},{5,4},{6,7},{7,6},{8,9},{9,8},{10,11... | collective-permute-start | bytes 12582920 | tf_op jit(solution)/shard_map/ppermute | solution.py:488
  0.5 1.8 %shard_map.154 = (bf16[8,8320]{1,0:T(8,128)(2,1)S(1)}, bf16[8,8320]{1,0:T(8,128)(2,1)S(1)}, bf16[8,8320]{1,0:T(8,128)(2,1)S(1)}, bf16[8,8320]{1,0:T(8,128)(2,1)S(1)}) custom-call(bf16[16,8192]{1,0:T(8,128)(2,1)} %x_hbm.1, f32[1,8192]{1,0:T(1,128)} %bitcast.30, bf16[512,128]{1,0:T(8,128)(2,1)} %bitcast.25, bf16[512,128]{1,0:T(8,128)(2,1)} %bitcast.26, ...), custom_call_target="tpu_custom_call" | custom-call | tf_op jit(solution)/shard_map/pallas_call | solution.py:368
  2.3 2.6 %collective-permute-start = (bf16[8,8320]{1,0:T(8,128)(2,1)S(1)}, bf16[8,8320]{1,0:T(8,128)(2,1)S(1)}, u32[]{:S(2)}, u32[]{:S(2)}) collective-permute-start(bf16[8,8320]{1,0:T(8,128)(2,1)S(1)} %get-tuple-element.45), channel_id=1, source_target_pairs={{0,4},{1,9},{2,6},{3,11},{4,8},{5,13},{6,10},{7,15},{8,12},{9,1},{... | collective-permute-start | bytes 399368 | tf_op jit(solution)/shard_map/ppermute | solution.py:484
  4.9 2.5 %collective-permute-start.1 = (bf16[8,8320]{1,0:T(8,128)(2,1)S(1)}, bf16[8,8320]{1,0:T(8,128)(2,1)S(1)}, u32[]{:S(2)}, u32[]{:S(2)}) collective-permute-start(bf16[8,8320]{1,0:T(8,128)(2,1)S(1)} %get-tuple-element.53), channel_id=1, source_target_pairs={{0,6},{1,11},{2,8},{3,13},{4,10},{5,15},{6,12},{7,1},{8,14},{9,3},... | collective-permute-start | bytes 399368 | tf_op jit(solution)/shard_map/ppermute | solution.py:484
  7.4 1.5 %collective-permute-start.2 = (bf16[8,8320]{1,0:T(8,128)(2,1)S(1)}, bf16[8,8320]{1,0:T(8,128)(2,1)S(1)}, u32[]{:S(2)}, u32[]{:S(2)}) collective-permute-start(bf16[8,8320]{1,0:T(8,128)(2,1)S(1)} %get-tuple-element.54), channel_id=1, source_target_pairs={{0,2},{1,15},{2,4},{3,1},{4,6},{5,3},{6,8},{7,5},{8,10},{9,7},{10,... | collective-permute-start | bytes 399368 | tf_op jit(solution)/shard_map/ppermute | solution.py:484
  9.0 0.7 %collective-permute-start.3 = (bf16[8,8320]{1,0:T(8,128)(2,1)S(1)}, bf16[8,8320]{1,0:T(8,128)(2,1)S(1)}, u32[]{:S(2)}, u32[]{:S(2)}) collective-permute-start(bf16[8,8320]{1,0:T(8,128)(2,1)S(1)} %get-tuple-element.55), channel_id=1, source_target_pairs={{0,0},{1,13},{2,2},{3,15},{4,4},{5,1},{6,6},{7,3},{8,8},{9,5},{10,... | collective-permute-start | bytes 399368 | tf_op jit(solution)/shard_map/ppermute | solution.py:484
  9.6 3.6 %shard_map.155 = (bf16[8192,256]{1,0:T(8,128)(2,1)S(1)}, bf16[448,4096]{1,0:T(8,128)(2,1)S(1)}, bf16[64,4736]{1,0:T(8,128)(2,1)S(1)}) custom-call(bf16[8192,256]{1,0:T(8,128)(2,1)} %wq_hbm, bf16[64,8192]{1,0:T(8,128)(2,1)} %bitcast.22, bf16[64,8192]{1,0:T(8,128)(2,1)} %bitcast.23, bf16[192,4096]{1,0:T(8,128)(2,1)} %bitcast.21, bf16[64,256]{1,0:T(8,128)(2,1)} %bitcast.27, ...), custom_call_target="tpu_custom_call" | custom-call | bytes 7864320 | tf_op jit(solution)/shard_map/pallas_call | solution.py:368
  13.2 0.0 collective-permute-done.refs_0_
  13.2 0.0 copy-start.1
  13.2 0.0 copy-start.2
  13.2 0.0 copy-start
  13.2 3.1 %collective-permute-start.4 = (bf16[8,8320]{1,0:T(8,128)(2,1)S(1)}, bf16[8,8320]{1,0:T(8,128)(2,1)S(1)}, u32[]{:S(2)}, u32[]{:S(2)}) collective-permute-start(bf16[8,8320]{1,0:T(8,128)(2,1)S(1)} %collective-permute-done.refs_0_), channel_id=1, source_target_pairs={{0,1},{1,0},{2,3},{3,2},{4,5},{5,4},{6,7},{7,6},{8,9},{9,8},{10,11... | collective-permute-start | bytes 399368 | tf_op jit(solution)/shard_map/ppermute | solution.py:487
  16.3 1.7 %collective-permute-done.1.refs_1_ = bf16[8,8320]{1,0:T(8,128)(2,1)S(1)} collective-permute-done((bf16[8,8320]{1,0:T(8,128)(2,1)S(1)}, bf16[8,8320]{1,0:T(8,128)(2,1)S(1)}, u32[]{:S(2)}, u32[]{:S(2)}) %collective-permute-start.1) | collective-permute-done | bytes 133152 | tf_op jit(solution)/shard_map/ppermute | solution.py:484
  18.0 0.0 collective-permute-start.5
  18.0 0.0 collective-permute-done.2.refs_2_
  18.0 0.5 %collective-permute-start.6 = (bf16[8,8320]{1,0:T(8,128)(2,1)S(1)}, bf16[8,8320]{1,0:T(8,128)(2,1)S(1)}, u32[]{:S(2)}, u32[]{:S(2)}) collective-permute-start(bf16[8,8320]{1,0:T(8,128)(2,1)S(1)} %collective-permute-done.2.refs_2_), channel_id=1, source_target_pairs={{0,1},{1,0},{2,3},{3,2},{4,5},{5,4},{6,7},{7,6},{8,9},{9,8},{10,11... | collective-permute-start | bytes 399368 | tf_op jit(solution)/shard_map/ppermute | solution.py:487
  18.5 0.0 collective-permute-done.3.refs_3_
  18.5 0.1 collective-permute-start.7
  18.6 0.0 collective-permute-done.4.refs_4_
  18.6 0.8 %collective-permute-done.5.refs_5_ = bf16[8,8320]{1,0:T(8,128)(2,1)S(1)} collective-permute-done((bf16[8,8320]{1,0:T(8,128)(2,1)S(1)}, bf16[8,8320]{1,0:T(8,128)(2,1)S(1)}, u32[]{:S(2)}, u32[]{:S(2)}) %collective-permute-start.5) | collective-permute-done | bytes 133152 | tf_op jit(solution)/shard_map/ppermute | solution.py:487
  19.4 0.2 collective-permute-done.6.refs_6_
  19.5 0.3 collective-permute-done.7.refs_7_
  19.9 1.9 %shard_map.157 = (f32[16,640]{1,0:T(8,128)S(1)}, f32[16,640]{1,0:T(8,128)S(1)}) custom-call(bf16[8,8320]{1,0:T(8,128)(2,1)S(1)} %collective-permute-done.refs_0_, bf16[8,8320]{1,0:T(8,128)(2,1)S(1)} %collective-permute-done.1.refs_1_, bf16[8,8320]{1,0:T(8,128)(2,1)S(1)} %collective-permute-done.2.refs_2_, ...), custom_call_target="tpu_custom_call" | custom-call | tf_op jit(solution)/shard_map/pallas_call | solution.py:368
  21.8 0.3 collective-permute-start.9
  22.0 0.3 collective-permute-start.8
  22.3 0.3 shard_map.156
  22.6 1.3 %collective-permute-done.8.theirs_ref = f32[16,640]{1,0:T(8,128)S(1)} collective-permute-done((f32[16,640]{1,0:T(8,128)S(1)}, f32[16,640]{1,0:T(8,128)S(1)}, u32[]{:S(2)}, u32[]{:S(2)}) %collective-permute-start.8) | collective-permute-done | bytes 40992 | tf_op jit(solution)/shard_map/ppermute | solution.py:497
  23.9 0.0 collective-permute-done.9.small_other_ref
  23.9 0.9 %shard_map.158.attended_ref = bf16[16,512]{1,0:T(8,128)(2,1)S(1)} custom-call(f32[16,640]{1,0:T(8,128)S(1)} %get-tuple-element.62.mine_ref, f32[16,640]{1,0:T(8,128)S(1)} %collective-permute-done.8.theirs_ref, bf16[64,4736]{1,0:T(8,128)(2,1)S(1)} %get-tuple-element.64.small_ref, bf16[64,4736]{1,0:T(8,128)(2,1)S(1)} %collective-permute-done.9.small_other_ref, ...), custom_call_target="tpu_custom_call" | custom-call | tf_op jit(solution)/shard_map/pallas_call | solution.py:368
  24.8 0.0 collective-permute-done.10.wo_other_ref
  24.8 1.5 %shard_map.159 = (bf16[8,4096]{1,0:T(8,128)(2,1)S(1)}, bf16[8,4096]{1,0:T(8,128)(2,1)S(1)}, bf16[8,4096]{1,0:T(8,128)(2,1)S(1)}, bf16[8,4096]{1,0:T(8,128)(2,1)S(1)}) custom-call(bf16[16,512]{1,0:T(8,128)(2,1)S(1)} %shard_map.158.attended_ref, bf16[256,8192]{1,0:T(8,128)(2,1)S(1)} %copy-done, bf16[256,8192]{1,0:T(8,128)(2,1)S(1)} %collective-permute-done.10.wo_other_ref, ...), custom_call_target="tpu_custom_call" | custom-call | tf_op jit(solution)/shard_map/pallas_call | solution.py:368
  26.3 4.2 %collective-permute-start.13 = (bf16[8,4096]{1,0:T(8,128)(2,1)S(1)}, bf16[8,4096]{1,0:T(8,128)(2,1)S(1)}, u32[]{:S(2)}, u32[]{:S(2)}) collective-permute-start(bf16[8,4096]{1,0:T(8,128)(2,1)S(1)} %get-tuple-element.72), channel_id=1, source_target_pairs={{2,0},{15,1},{4,2},{1,3},{6,4},{3,5},{8,6},{5,7},{10,8},{7,9},{12,... | collective-permute-start | bytes 196616 | tf_op jit(solution)/shard_map/ppermute | solution.py:514
  30.6 0.7 %collective-permute-start.14 = (bf16[8,4096]{1,0:T(8,128)(2,1)S(1)}, bf16[8,4096]{1,0:T(8,128)(2,1)S(1)}, u32[]{:S(2)}, u32[]{:S(2)}) collective-permute-start(bf16[8,4096]{1,0:T(8,128)(2,1)S(1)} %get-tuple-element.73), channel_id=1, source_target_pairs={{0,0},{13,1},{2,2},{15,3},{4,4},{1,5},{6,6},{3,7},{8,8},{5,9},{10,... | collective-permute-start | bytes 196616 | tf_op jit(solution)/shard_map/ppermute | solution.py:514
  31.2 0.8 %collective-permute-start.12 = (bf16[8,4096]{1,0:T(8,128)(2,1)S(1)}, bf16[8,4096]{1,0:T(8,128)(2,1)S(1)}, u32[]{:S(2)}, u32[]{:S(2)}) collective-permute-start(bf16[8,4096]{1,0:T(8,128)(2,1)S(1)} %get-tuple-element.71), channel_id=1, source_target_pairs={{6,0},{11,1},{8,2},{13,3},{10,4},{15,5},{12,6},{1,7},{14,8},{3,9},... | collective-permute-start | bytes 196616 | tf_op jit(solution)/shard_map/ppermute | solution.py:514
  32.1 0.0 collective-permute-start.11
  32.1 0.4 %collective-permute-done.13.refs_2_ = bf16[8,4096]{1,0:T(8,128)(2,1)S(1)} collective-permute-done((bf16[8,4096]{1,0:T(8,128)(2,1)S(1)}, bf16[8,4096]{1,0:T(8,128)(2,1)S(1)}, u32[]{:S(2)}, u32[]{:S(2)}) %collective-permute-start.13) | collective-permute-done | bytes 65568 | tf_op jit(solution)/shard_map/ppermute | solution.py:514
  32.5 0.0 collective-permute-done.14.refs_3_
  32.5 2.6 %collective-permute-start.17 = (bf16[8,4096]{1,0:T(8,128)(2,1)S(1)}, bf16[8,4096]{1,0:T(8,128)(2,1)S(1)}, u32[]{:S(2)}, u32[]{:S(2)}) collective-permute-start(bf16[8,4096]{1,0:T(8,128)(2,1)S(1)} %collective-permute-done.13.refs_2_), channel_id=1, source_target_pairs={{0,1},{1,0},{2,3},{3,2},{4,5},{5,4},{6,7},{7,6},{8,9},{9,8},{10,11... | collective-permute-start | bytes 196616 | tf_op jit(solution)/shard_map/ppermute | solution.py:520
  35.1 1.4 %collective-permute-done.12.refs_1_ = bf16[8,4096]{1,0:T(8,128)(2,1)S(1)} collective-permute-done((bf16[8,4096]{1,0:T(8,128)(2,1)S(1)}, bf16[8,4096]{1,0:T(8,128)(2,1)S(1)}, u32[]{:S(2)}, u32[]{:S(2)}) %collective-permute-start.12) | collective-permute-done | bytes 65568 | tf_op jit(solution)/shard_map/ppermute | solution.py:514
  36.5 0.0 collective-permute-start.16
  36.5 0.0 collective-permute-done.11.refs_0_
  36.5 0.5 %collective-permute-start.15 = (bf16[8,4096]{1,0:T(8,128)(2,1)S(1)}, bf16[8,4096]{1,0:T(8,128)(2,1)S(1)}, u32[]{:S(2)}, u32[]{:S(2)}) collective-permute-start(bf16[8,4096]{1,0:T(8,128)(2,1)S(1)} %collective-permute-done.11.refs_0_), channel_id=1, source_target_pairs={{0,1},{1,0},{2,3},{3,2},{4,5},{5,4},{6,7},{7,6},{8,9},{9,8},{10,11... | collective-permute-start | bytes 196616 | tf_op jit(solution)/shard_map/ppermute | solution.py:520
  37.1 0.0 collective-permute-start.18
  37.1 0.0 collective-permute-done.17.refs_6_
  37.1 0.7 %collective-permute-done.16.refs_5_ = bf16[8,4096]{1,0:T(8,128)(2,1)S(1)} collective-permute-done((bf16[8,4096]{1,0:T(8,128)(2,1)S(1)}, bf16[8,4096]{1,0:T(8,128)(2,1)S(1)}, u32[]{:S(2)}, u32[]{:S(2)}) %collective-permute-start.16) | collective-permute-done | bytes 65568 | tf_op jit(solution)/shard_map/ppermute | solution.py:520
  37.8 0.2 collective-permute-done.15.refs_4_
  38.0 0.4 collective-permute-done.18.refs_7_
  38.3 0.8 %shard_map.160 = bf16[16,4096]{1,0:T(8,128)(2,1)} custom-call(bf16[16,64]{1,0:T(8,128)(2,1)S(1)} %get-tuple-element.56.place_ref, bf16[8,4096]{1,0:T(8,128)(2,1)S(1)} %collective-permute-done.11.refs_0_, bf16[8,4096]{1,0:T(8,128)(2,1)S(1)} %collective-permute-done.12.refs_1_, bf16[8,4096]{1,0:T(8,128)(2,1)S(1)} %collective-permute-done.13.refs_2_, ...), custom_call_target="tpu_custom_call" | custom-call | tf_op jit(solution)/shard_map/pallas_call | solution.py:368
  (3 shorter events, 0.0 us)
Async XLA Ops:
  0.0 24.8 %collective-permute-start.10 = (bf16[256,8192]{1,0:T(8,128)(2,1)}, bf16[256,8192]{1,0:T(8,128)(2,1)S(1)}, u32[]{:S(2)}, u32[]{:S(2)}) collective-permute-start(bf16[256,8192]{1,0:T(8,128)(2,1)} %wo_ref.1), channel_id=1, source_target_pairs={{0,1},{1,0},{2,3},{3,2},{4,5},{5,4},{6,7},{7,6},{8,9},{9,8},{10,11... | collective-permute-start | bytes 12582920 | tf_op jit(solution)/shard_map/ppermute | solution.py:488
  2.3 10.9 %collective-permute-start = (bf16[8,8320]{1,0:T(8,128)(2,1)S(1)}, bf16[8,8320]{1,0:T(8,128)(2,1)S(1)}, u32[]{:S(2)}, u32[]{:S(2)}) collective-permute-start(bf16[8,8320]{1,0:T(8,128)(2,1)S(1)} %get-tuple-element.45), channel_id=1, source_target_pairs={{0,4},{1,9},{2,6},{3,11},{4,8},{5,13},{6,10},{7,15},{8,12},{9,1},{... | collective-permute-start | bytes 399368 | tf_op jit(solution)/shard_map/ppermute | solution.py:484
  4.9 13.1 %collective-permute-start.1 = (bf16[8,8320]{1,0:T(8,128)(2,1)S(1)}, bf16[8,8320]{1,0:T(8,128)(2,1)S(1)}, u32[]{:S(2)}, u32[]{:S(2)}) collective-permute-start(bf16[8,8320]{1,0:T(8,128)(2,1)S(1)} %get-tuple-element.53), channel_id=1, source_target_pairs={{0,6},{1,11},{2,8},{3,13},{4,10},{5,15},{6,12},{7,1},{8,14},{9,3},... | collective-permute-start | bytes 399368 | tf_op jit(solution)/shard_map/ppermute | solution.py:484
  7.4 10.6 %collective-permute-start.2 = (bf16[8,8320]{1,0:T(8,128)(2,1)S(1)}, bf16[8,8320]{1,0:T(8,128)(2,1)S(1)}, u32[]{:S(2)}, u32[]{:S(2)}) collective-permute-start(bf16[8,8320]{1,0:T(8,128)(2,1)S(1)} %get-tuple-element.54), channel_id=1, source_target_pairs={{0,2},{1,15},{2,4},{3,1},{4,6},{5,3},{6,8},{7,5},{8,10},{9,7},{10,... | collective-permute-start | bytes 399368 | tf_op jit(solution)/shard_map/ppermute | solution.py:484
  9.0 9.5 %collective-permute-start.3 = (bf16[8,8320]{1,0:T(8,128)(2,1)S(1)}, bf16[8,8320]{1,0:T(8,128)(2,1)S(1)}, u32[]{:S(2)}, u32[]{:S(2)}) collective-permute-start(bf16[8,8320]{1,0:T(8,128)(2,1)S(1)} %get-tuple-element.55), channel_id=1, source_target_pairs={{0,0},{1,13},{2,2},{3,15},{4,4},{5,1},{6,6},{7,3},{8,8},{9,5},{10,... | collective-permute-start | bytes 399368 | tf_op jit(solution)/shard_map/ppermute | solution.py:484
  13.2 9.1 %copy-start.1 = (s32[16,1]{0,1:T(1,128)S(1)}, s32[16,1]{0,1:T(1,128)}, u32[]{:S(2)}) copy-start(s32[16,1]{0,1:T(1,128)} %param.24) | copy-start | bytes 196
  13.2 9.1 %copy-start.2 = (s32[8]{0:T(128)S(1)}, s32[8]{0:T(128)}, u32[]{:S(2)}) copy-start(s32[8]{0:T(128)} %param.25) | copy-start | bytes 100
  13.2 11.6 %copy-start = (bf16[256,8192]{1,0:T(8,128)(2,1)S(1)}, bf16[256,8192]{1,0:T(8,128)(2,1)}, u32[]{:S(2)}) copy-start(bf16[256,8192]{1,0:T(8,128)(2,1)} %wo_ref.1) | copy-start | bytes 12582916
  13.2 5.3 %collective-permute-start.4 = (bf16[8,8320]{1,0:T(8,128)(2,1)S(1)}, bf16[8,8320]{1,0:T(8,128)(2,1)S(1)}, u32[]{:S(2)}, u32[]{:S(2)}) collective-permute-start(bf16[8,8320]{1,0:T(8,128)(2,1)S(1)} %collective-permute-done.refs_0_), channel_id=1, source_target_pairs={{0,1},{1,0},{2,3},{3,2},{4,5},{5,4},{6,7},{7,6},{8,9},{9,8},{10,11... | collective-permute-start | bytes 399368 | tf_op jit(solution)/shard_map/ppermute | solution.py:487
  18.0 1.4 %collective-permute-start.5 = (bf16[8,8320]{1,0:T(8,128)(2,1)S(1)}, bf16[8,8320]{1,0:T(8,128)(2,1)S(1)}, u32[]{:S(2)}, u32[]{:S(2)}) collective-permute-start(bf16[8,8320]{1,0:T(8,128)(2,1)S(1)} %collective-permute-done.1.refs_1_), channel_id=1, source_target_pairs={{0,1},{1,0},{2,3},{3,2},{4,5},{5,4},{6,7},{7,6},{8,9},{9,8},{10,11... | collective-permute-start | bytes 399368 | tf_op jit(solution)/shard_map/ppermute | solution.py:487
  18.0 1.5 %collective-permute-start.6 = (bf16[8,8320]{1,0:T(8,128)(2,1)S(1)}, bf16[8,8320]{1,0:T(8,128)(2,1)S(1)}, u32[]{:S(2)}, u32[]{:S(2)}) collective-permute-start(bf16[8,8320]{1,0:T(8,128)(2,1)S(1)} %collective-permute-done.2.refs_2_), channel_id=1, source_target_pairs={{0,1},{1,0},{2,3},{3,2},{4,5},{5,4},{6,7},{7,6},{8,9},{9,8},{10,11... | collective-permute-start | bytes 399368 | tf_op jit(solution)/shard_map/ppermute | solution.py:487
  18.5 1.4 %collective-permute-start.7 = (bf16[8,8320]{1,0:T(8,128)(2,1)S(1)}, bf16[8,8320]{1,0:T(8,128)(2,1)S(1)}, u32[]{:S(2)}, u32[]{:S(2)}) collective-permute-start(bf16[8,8320]{1,0:T(8,128)(2,1)S(1)} %collective-permute-done.3.refs_3_), channel_id=1, source_target_pairs={{0,1},{1,0},{2,3},{3,2},{4,5},{5,4},{6,7},{7,6},{8,9},{9,8},{10,11... | collective-permute-start | bytes 399368 | tf_op jit(solution)/shard_map/ppermute | solution.py:487
  21.8 2.2 %collective-permute-start.9 = (bf16[64,4736]{1,0:T(8,128)(2,1)S(1)}, bf16[64,4736]{1,0:T(8,128)(2,1)S(1)}, u32[]{:S(2)}, u32[]{:S(2)}) collective-permute-start(bf16[64,4736]{1,0:T(8,128)(2,1)S(1)} %get-tuple-element.64.small_ref), channel_id=1, source_target_pairs={{0,1},{1,0},{2,3},{3,2},{4,5},{5,4},{6,7},{7,6},{8,9},{9,8},{10,11... | collective-permute-start | bytes 1818632 | tf_op jit(solution)/shard_map/ppermute | solution.py:498
  22.0 1.9 %collective-permute-start.8 = (f32[16,640]{1,0:T(8,128)S(1)}, f32[16,640]{1,0:T(8,128)S(1)}, u32[]{:S(2)}, u32[]{:S(2)}) collective-permute-start(f32[16,640]{1,0:T(8,128)S(1)} %get-tuple-element.63), channel_id=1, source_target_pairs={{0,1},{1,0},{2,3},{3,2},{4,5},{5,4},{6,7},{7,6},{8,9},{9,8},{10,11... | collective-permute-start | bytes 122888 | tf_op jit(solution)/shard_map/ppermute | solution.py:497
  26.3 6.2 %collective-permute-start.13 = (bf16[8,4096]{1,0:T(8,128)(2,1)S(1)}, bf16[8,4096]{1,0:T(8,128)(2,1)S(1)}, u32[]{:S(2)}, u32[]{:S(2)}) collective-permute-start(bf16[8,4096]{1,0:T(8,128)(2,1)S(1)} %get-tuple-element.72), channel_id=1, source_target_pairs={{2,0},{15,1},{4,2},{1,3},{6,4},{3,5},{8,6},{5,7},{10,8},{7,9},{12,... | collective-permute-start | bytes 196616 | tf_op jit(solution)/shard_map/ppermute | solution.py:514
  30.6 1.9 %collective-permute-start.14 = (bf16[8,4096]{1,0:T(8,128)(2,1)S(1)}, bf16[8,4096]{1,0:T(8,128)(2,1)S(1)}, u32[]{:S(2)}, u32[]{:S(2)}) collective-permute-start(bf16[8,4096]{1,0:T(8,128)(2,1)S(1)} %get-tuple-element.73), channel_id=1, source_target_pairs={{0,0},{13,1},{2,2},{15,3},{4,4},{1,5},{6,6},{3,7},{8,8},{5,9},{10,... | collective-permute-start | bytes 196616 | tf_op jit(solution)/shard_map/ppermute | solution.py:514
  31.2 5.3 %collective-permute-start.12 = (bf16[8,4096]{1,0:T(8,128)(2,1)S(1)}, bf16[8,4096]{1,0:T(8,128)(2,1)S(1)}, u32[]{:S(2)}, u32[]{:S(2)}) collective-permute-start(bf16[8,4096]{1,0:T(8,128)(2,1)S(1)} %get-tuple-element.71), channel_id=1, source_target_pairs={{6,0},{11,1},{8,2},{13,3},{10,4},{15,5},{12,6},{1,7},{14,8},{3,9},... | collective-permute-start | bytes 196616 | tf_op jit(solution)/shard_map/ppermute | solution.py:514
  32.1 4.5 %collective-permute-start.11 = (bf16[8,4096]{1,0:T(8,128)(2,1)S(1)}, bf16[8,4096]{1,0:T(8,128)(2,1)S(1)}, u32[]{:S(2)}, u32[]{:S(2)}) collective-permute-start(bf16[8,4096]{1,0:T(8,128)(2,1)S(1)} %get-tuple-element.70), channel_id=1, source_target_pairs={{4,0},{9,1},{6,2},{11,3},{8,4},{13,5},{10,6},{15,7},{12,8},{1,9},{... | collective-permute-start | bytes 196616 | tf_op jit(solution)/shard_map/ppermute | solution.py:514
  32.5 4.6 %collective-permute-start.17 = (bf16[8,4096]{1,0:T(8,128)(2,1)S(1)}, bf16[8,4096]{1,0:T(8,128)(2,1)S(1)}, u32[]{:S(2)}, u32[]{:S(2)}) collective-permute-start(bf16[8,4096]{1,0:T(8,128)(2,1)S(1)} %collective-permute-done.13.refs_2_), channel_id=1, source_target_pairs={{0,1},{1,0},{2,3},{3,2},{4,5},{5,4},{6,7},{7,6},{8,9},{9,8},{10,11... | collective-permute-start | bytes 196616 | tf_op jit(solution)/shard_map/ppermute | solution.py:520
  36.5 1.3 %collective-permute-start.16 = (bf16[8,4096]{1,0:T(8,128)(2,1)S(1)}, bf16[8,4096]{1,0:T(8,128)(2,1)S(1)}, u32[]{:S(2)}, u32[]{:S(2)}) collective-permute-start(bf16[8,4096]{1,0:T(8,128)(2,1)S(1)} %collective-permute-done.12.refs_1_), channel_id=1, source_target_pairs={{0,1},{1,0},{2,3},{3,2},{4,5},{5,4},{6,7},{7,6},{8,9},{9,8},{10,11... | collective-permute-start | bytes 196616 | tf_op jit(solution)/shard_map/ppermute | solution.py:520
  36.5 1.4 %collective-permute-start.15 = (bf16[8,4096]{1,0:T(8,128)(2,1)S(1)}, bf16[8,4096]{1,0:T(8,128)(2,1)S(1)}, u32[]{:S(2)}, u32[]{:S(2)}) collective-permute-start(bf16[8,4096]{1,0:T(8,128)(2,1)S(1)} %collective-permute-done.11.refs_0_), channel_id=1, source_target_pairs={{0,1},{1,0},{2,3},{3,2},{4,5},{5,4},{6,7},{7,6},{8,9},{9,8},{10,11... | collective-permute-start | bytes 196616 | tf_op jit(solution)/shard_map/ppermute | solution.py:520
  37.1 1.3 %collective-permute-start.18 = (bf16[8,4096]{1,0:T(8,128)(2,1)S(1)}, bf16[8,4096]{1,0:T(8,128)(2,1)S(1)}, u32[]{:S(2)}, u32[]{:S(2)}) collective-permute-start(bf16[8,4096]{1,0:T(8,128)(2,1)S(1)} %collective-permute-done.14.refs_3_), channel_id=1, source_target_pairs={{0,1},{1,0},{2,3},{3,2},{4,5},{5,4},{6,7},{7,6},{8,9},{9,8},{10,11... | collective-permute-start | bytes 196616 | tf_op jit(solution)/shard_map/ppermute | solution.py:520
